TPU v7x, 256 devices: a whole 4x4x8 slice. The times are simulated.
256 devices in a mesh: rel: 8 (over z_lo, core), ent: 32 (over x, z_hi, y).
Axes of the slice: x: 4, y: 4, z: 8 (z_hi: 2, z_lo: 4; z = z_hi * 4 + z_lo), core: 2. Of those that a mesh axis runs over, the one named last changes fastest.
Arguments:
- facts: bfloat16 [64, 4096, 4096], P('rel', 'ent'), may hold values from -6 to 6
- observed: int32 [64, 4096, 316], P('rel', 'ent'), may hold values from 0 to 8191
- factors: bfloat16 [4096, 128], P('ent'), may hold values from -0.59765625 to 0.59765625
- cores: bfloat16 [64, 128, 128], P('rel'), may hold values from -6 to 6
Outputs:
- grad_factors: float32 [4096, 128], P('ent')
- grad_cores: float32 [64, 128, 128], P('rel')
All inputs are finite; a program needn't handle non-finite values.
Results may differ from a plain program's by a relative error of at most 0.0008.
Values may be sent and summed in bfloat16 or wider, within the bound.
A program may use at most 128 MiB of HBM per device.

v0:
```python
import jax
import jax.numpy as jnp
from jax import lax
from jax.sharding import PartitionSpec as P


def unpack(words, count):
    shifts = jnp.arange(13, dtype=jnp.int32)
    bits = jnp.bitwise_and(jnp.right_shift(words[..., None], shifts), 1)
    flat = bits.reshape(words.shape[:-1] + (words.shape[-1] * 13,))
    return flat[..., :count].astype(jnp.bfloat16)


def per_device(facts, observed, factors, cores):
    n_all = facts.shape[2]
    rel_loc, ent_loc, rank = (cores.shape[0], factors.shape[0], factors.shape[1])
    n_rel = rel_loc * lax.axis_size("rel")
    mask = unpack(observed, n_all)
    left = jnp.einsum("ir,krs->kis", factors, cores, preferred_element_type=jnp.float32).astype(
        jnp.bfloat16
    )
    piece = lax.all_gather(factors, "ent", axis=0, tiled=True)
    right = jnp.einsum("js,krs->kjr", piece, cores, preferred_element_type=jnp.float32).astype(
        jnp.bfloat16
    )
    model = jnp.einsum("kis,js->kij", left, piece, preferred_element_type=jnp.float32)
    data = facts.astype(jnp.float32)
    marks = mask.astype(jnp.float32)
    err = (marks * (model - data)).astype(jnp.bfloat16)
    own_rows = jnp.einsum("kij,kjr->ir", err, right, preferred_element_type=jnp.float32)
    block = jnp.einsum("kij,kis->js", err, left, preferred_element_type=jnp.float32)
    all_rows = block
    pull_sum = jnp.einsum("kij,js->kis", err, piece, preferred_element_type=jnp.float32)
    own_rows, all_rows, pull_sum = (own_rows, all_rows, pull_sum)
    offset = lax.axis_index("ent") * ent_loc
    mine = lax.dynamic_slice_in_dim(all_rows, offset, ent_loc, 0)
    partial_value = lax.dynamic_update_slice_in_dim(all_rows, mine + own_rows, offset, 0)
    shared = lax.psum_scatter(partial_value, "ent", scatter_dimension=0, tiled=True)
    owned = lax.psum(shared, "rel")
    grad_factors = owned / jnp.sqrt(jnp.float32(n_all * n_rel))
    pull = pull_sum.astype(jnp.bfloat16)
    core_part = jnp.einsum("ir,kis->krs", factors, pull, preferred_element_type=jnp.float32)
    core_grad = lax.psum(core_part, "ent")
    grad_cores = core_grad * (rank / n_all)
    return (grad_factors, grad_cores)


def solution(mesh):
    return jax.shard_map(
        per_device,
        mesh=mesh,
        in_specs=(
            P("rel", "ent", None),
            P("rel", "ent", None),
            P("ent", None),
            P("rel", None, None),
        ),
        out_specs=(P("ent", None), P("rel", None, None)),
        check_vma=False,
    )
```

profile of v0, /device:TPU:2, one launch (start us, length us, event | category | flops | bytes accessed | tf_op | source)
XLA Modules:
  0.0 909.6 jit_solution(7252655520066823902)
XLA Ops:
  7.2 0.0 copy-start
  7.2 0.0 all-gather.2.cloned.1.call-start
  7.2 0.7 all-gather.2.cloned.1.call-update
  7.9 0.0 reduce-scatter.2.cloned.1.call-start
  8.0 12.1 %copy.20 = bf16[8,128,4096]{1,0,2:T(8,128)(2,1)} copy(bf16[8,128,4096]{2,1,0:T(8,128)(2,1)} %param.4) | data formatting | bytes 16777216 | tf_op args[0]
  20.1 0.2 shift_right_arithmetic.23
  20.3 0.0 copy-start.7
  20.3 0.3 fusion.2
  20.6 0.0 copy-start.4
  20.6 74.4 %all-gather.2.cloned.1.call-done = bf16[4096,128]{1,0:T(8,128)(2,1)} async-done(((bf16[128,128]{1,0:T(8,128)(2,1)}), bf16[4096,128]{1,0:T(8,128)(2,1)}) %all-gather.2.cloned.1.call-update) | async-done | bytes 1048592 | tf_op jit(solution)/shard_map/all_gather | solution.py:22
  95.0 9.3 %fusion.8 = f32[8,128,4096]{2,1,0:T(8,128)} fusion(bf16[8,128,128]{1,2,0:T(8,128)(2,1)S(1)} %fusion.2, bf16[4096,128]{1,0:T(8,128)(2,1)} %all-gather.2.cloned.1.call-done), kind=kOutput, calls=%fused_computation.15 | convolution fusion | flops 1073741824 | bytes 18087936 | tf_op jit(solution)/shard_map/kis,js->kij/dot_general | solution.py:26
  104.4 17.6 %copy.21 = f32[8,128,4096]{1,0,2:T(8,128)} copy(f32[8,128,4096]{2,1,0:T(8,128)} %fusion.8) | data formatting | bytes 33554432 | tf_op jit(solution)/shard_map/kis,js->kij/dot_general | solution.py:26
  122.0 1.1 shift_right_arithmetic.20
  123.1 15.2 %multiply_convert_fusion = bf16[8,128,4096]{1,0,2:T(8,128)(2,1)} fusion(f32[8,128,4096]{1,0,2:T(8,128)} %copy.21, bf16[8,128,4096]{1,0,2:T(8,128)(2,1)} %copy.20, s32[8,128,4108]{1,0,2:T(8,128)S(1)} %bitcast.36, s32[4096]{0:T(1024)S(1)} %slice-done), kind=kLoop, calls=%fused_computation.3 | loop fusion | flops 33554432 | bytes 50348032 | tf_op jit(solution)/shard_map/convert_element_type | solution.py:29
  138.2 11.9 %copy.26 = bf16[8,128,4096]{2,1,0:T(8,128)(2,1)} copy(bf16[8,128,4096]{1,0,2:T(8,128)(2,1)} %multiply_convert_fusion) | data formatting | bytes 16777216 | tf_op jit(solution)/shard_map/convert_element_type | solution.py:29
  150.1 5.8 convolution_bitcast_fusion
  156.0 5.6 convert_bitcast_fusion
  161.6 12.0 %copy.33 = bf16[8,4096,128]{2,0,1:T(8,128)(2,1)} copy(bf16[8,4096,128]{1,2,0:T(8,128)(2,1)} %convert_bitcast_fusion) | data formatting | bytes 16777216 | tf_op jit(solution)/shard_map/convert_element_type | solution.py:23
  173.5 8.3 fusion.4
  181.9 1.4 copy-done.2
  183.2 0.0 reduce-scatter.2.cloned.1.call-update
  183.2 0.0 all-reduce.5.cloned.1.call-start
  183.3 6.7 convolution_bitcast_fusion.1
  190.0 0.0 all-reduce.5.cloned.1.call-update
  190.1 0.0 all-reduce.3.cloned.1.call-start
  190.1 197.8 %reduce-scatter.2.cloned.1.call-done = f32[128,128]{1,0:T(8,128)} async-done(((f32[4096,128]{1,0:T(8,128)}), f32[128,128]{1,0:T(8,128)}) %reduce-scatter.2.cloned.1.call-update) | async-done | bytes 65552 | tf_op jit(solution)/shard_map/reduce_scatter | solution.py:38
  387.9 0.0 all-reduce.3.cloned.1.call-update
  387.9 425.7 %all-reduce.5.cloned.1.call-done = f32[8,128,128]{1,2,0:T(8,128)} async-done(((f32[8,128,128]{1,2,0:T(8,128)}), f32[8,128,128]{1,2,0:T(8,128)}) %all-reduce.5.cloned.1.call-update) | async-done | bytes 524304 | tf_op jit(solution)/shard_map/psum | solution.py:43
  813.6 1.1 broadcast_multiply_fusion
  814.7 1.0 copy.28
  815.7 85.9 %all-reduce.3.cloned.1.call-done = f32[128,128]{1,0:T(8,128)} async-done(((f32[128,128]{1,0:T(8,128)}), f32[128,128]{1,0:T(8,128)}) %all-reduce.3.cloned.1.call-update) | async-done | bytes 65552 | tf_op jit(solution)/shard_map/psum | solution.py:39
  901.6 1.5 broadcast_multiply_fusion.1
  (15 shorter events, 0.0 us)
Async XLA Ops:
  7.2 13.2 %copy-start = (bf16[8,128,128]{2,1,0:T(8,128)(2,1)S(1)}, bf16[8,128,128]{2,1,0:T(8,128)(2,1)}, u32[]{:S(2)}) copy-start(bf16[8,128,128]{2,1,0:T(8,128)(2,1)} %param.7) | copy-start | bytes 786436
  7.2 87.8 %all-gather.2.cloned.1.call-start = ((), (), s32[]{:S(2)}) async-start(), calls=%async_computation.1 | async-start | bytes 1081344 | tf_op jit(solution)/shard_map/all_gather | solution.py:22
  7.9 380.0 %reduce-scatter.2.cloned.1.call-start = ((), (), s32[]{:S(2)}) async-start(), calls=%async_computation.2 | async-start | bytes 2162688 | tf_op jit(solution)/shard_map/reduce_scatter | solution.py:38
  8.0 12.4 %copy-start.6 = (bf16[128,128]{1,0:T(8,128)(2,1)S(1)}, bf16[128,128]{1,0:T(8,128)(2,1)}, u32[]{:S(2)}) copy-start(bf16[128,128]{1,0:T(8,128)(2,1)} %param.6) | copy-start | bytes 98308
  20.3 84.1 %copy-start.7 = (s32[4108]{0:T(1024)}, s32[4108]{0:T(1024)S(1)}, u32[]{:S(2)}) copy-start(s32[4108]{0:T(1024)S(1)} %shift_right_arithmetic.23) | copy-start | bytes 49300
  20.6 83.8 %copy-start.4 = (bf16[8,128,128]{1,2,0:T(8,128)(2,1)}, bf16[8,128,128]{1,2,0:T(8,128)(2,1)S(1)}, u32[]{:S(2)}) copy-start(bf16[8,128,128]{1,2,0:T(8,128)(2,1)S(1)} %fusion.2) | copy-start | bytes 786436
  104.4 17.6 %copy-start.5 = (s32[8,128,316]{1,0,2:T(8,128)S(1)}, s32[8,128,316]{1,0,2:T(8,128)}, u32[]{:S(2)}) copy-start(s32[8,128,316]{1,0,2:T(8,128)} %param.5) | copy-start | bytes 3883012
  122.0 1.1 slice-start
  150.1 5.9 copy-start.3
  173.5 729.6 %copy-start.1 = (bf16[8,128,128]{2,1,0:T(8,128)(2,1)S(1)}, bf16[8,128,128]{2,1,0:T(8,128)(2,1)}, u32[]{:S(2)}) copy-start(bf16[8,128,128]{2,1,0:T(8,128)(2,1)} %param.7) | copy-start | bytes 786436
  181.9 1.4 copy-start.2
  183.2 630.4 %all-reduce.5.cloned.1.call-start = ((), (), s32[]{:S(2)}) async-start(), calls=%async_computation.4 | async-start | bytes 1048576 | tf_op jit(solution)/shard_map/psum | solution.py:43
  190.1 711.6 %all-reduce.3.cloned.1.call-start = ((), (), s32[]{:S(2)}) async-start(), calls=%async_computation.3 | async-start | bytes 131072 | tf_op jit(solution)/shard_map/psum | solution.py:39
Sparse Core Ops, SparseCore 0:
  11.4 83.5 all-gather.1
  183.4 204.4 reduce-scatter.1
  391.2 422.3 all-reduce.4
  816.1 85.4 all-reduce.2
where the time goes:
time: 911 us; the launch traced here: 910 us
  waiting for transfers between devices  785 us (86%)
  local copies, waits for them, and re-layouts  57.2 us (6%)
  matrix products  36.1 us (4%)
  other arithmetic  17.7 us (2%)
  between operations  13.9 us (2%)
    psum x1, waiting for transfers between devices, per_device(): core_grad = lax.psum(core_part, 'ent')  426 us
    reduce_scatter x1, waiting for transfers between devices, per_device(): lax.psum_scatter(partial_value, 'ent', scatter_dimension=0, tiled=True)  198 us
    psum x1, waiting for transfers between devices, per_device(): owned = lax.psum(shared, 'rel')  85.9 us
    all_gather x1, waiting for transfers between devices, per_device(): piece = lax.all_gather(factors, 'ent', axis=0, tiled=True)  74.4 us
  transfers between devices with their start and end apart: 4, of which 4 were waited for; matrix products, arithmetic and copies ran while one was open for 2% of the time, Pallas kernels for 0%

commit v1 on v0

--- a/solution.py
+++ b/solution.py
@@ -19,7 +19,9 @@
     left = jnp.einsum("ir,krs->kis", factors, cores, preferred_element_type=jnp.float32).astype(
         jnp.bfloat16
     )
-    piece = lax.all_gather(factors, "ent", axis=0, tiled=True)
+    piece = jnp.concatenate(
+        lax.all_to_all(jnp.stack([factors] * lax.axis_size("ent")), "ent", 0, 0), axis=0
+    )
     right = jnp.einsum("js,krs->kjr", piece, cores, preferred_element_type=jnp.float32).astype(
         jnp.bfloat16
     )

time: 911 us -> 871 us (0.956)
  waiting for transfers between devices: 785 us -> 728 us
  starting transfers between devices: 0.16 us -> 14.4 us
    all_gather x1 -> x0, waiting for transfers between devices: 74.4 us -> none  [per_device(): piece = lax.all_gather(factors, 'ent', axis=0, tiled=True)]
    all_to_all x0 -> x1, starting transfers between devices: none -> 14.2 us  [per_device(): lax.all_to_all(jnp.stack([factors] * lax.axis_size('ent')), 'ent', 0, 0)]
    reduce_scatter x1, waiting for transfers between devices: 198 us -> 207 us  [per_device(): lax.psum_scatter(partial_value, 'ent', scatter_dimension=0, tiled=True)]
where the time goes in v1:
time: 871 us; the launch traced here: 869 us
  waiting for transfers between devices  728 us (84%)
  local copies, waits for them, and re-layouts  59.1 us (7%)
  matrix products  36.7 us (4%)
  other arithmetic  17.7 us (2%)
  starting transfers between devices  14.4 us (2%)
  between operations  13.8 us (2%)
    psum x1, waiting for transfers between devices, per_device(): core_grad = lax.psum(core_part, 'ent')  426 us
    reduce_scatter x1, waiting for transfers between devices, per_device(): lax.psum_scatter(partial_value, 'ent', scatter_dimension=0, tiled=True)  207 us
    psum x1, waiting for transfers between devices, per_device(): owned = lax.psum(shared, 'rel')  86.1 us
    dot_general x1, local copies, waits for them, and re-layouts, per_device(): jnp.einsum('kis,js->kij', left, piece, preferred_element_type=jnp.float32)  17.5 us
  transfers between devices with their start and end apart: 4, of which 4 were waited for; matrix products, arithmetic and copies ran while one was open for 2% of the time, Pallas kernels for 0%

profile of v1, /device:TPU:2, one launch (start us, length us, event | category | flops | bytes accessed | tf_op | source)
XLA Modules:
  0.0 869.5 jit_solution(11047226222290556841)
XLA Ops:
  7.2 0.0 copy-start
  7.2 2.0 stack.2
  9.2 14.2 %all-to-all-start = ((bf16[32,128,128]{2,1,0:T(8,128)(2,1)}), bf16[32,128,128]{2,1,0:T(8,128)(2,1)S(1)}, u32[]{:S(2)}, u32[]{:S(2)}) async-start(bf16[32,128,128]{2,1,0:T(8,128)(2,1)} %stack.2), calls=%async_computation | async-start | bytes 2097152 | tf_op jit(solution)/shard_map/all_to_all | solution.py:23
  23.4 0.0 reduce-scatter.2.cloned.1.call-start
  23.5 0.0 copy-start.2
  23.5 12.0 %copy.20 = bf16[8,128,4096]{1,0,2:T(8,128)(2,1)} copy(bf16[8,128,4096]{2,1,0:T(8,128)(2,1)} %param.4) | data formatting | bytes 16777216 | tf_op args[0]
  35.5 0.2 shift_right_arithmetic.23
  35.7 0.0 copy-start.3
  35.8 0.3 fusion.2
  36.0 8.7 %all-to-all-done = bf16[32,128,128]{2,1,0:T(8,128)(2,1)S(1)} async-done(((bf16[32,128,128]{2,1,0:T(8,128)(2,1)}), bf16[32,128,128]{2,1,0:T(8,128)(2,1)S(1)}, u32[]{:S(2)}, u32[]{:S(2)}) %all-to-all-start) | async-done | bytes 1048608 | tf_op jit(solution)/shard_map/all_to_all | solution.py:23
  44.8 5.6 convert_bitcast_fusion
  50.3 8.1 fusion.7
  58.4 0.0 copy-done.3
  58.4 17.5 %copy.21 = f32[8,128,4096]{1,0,2:T(8,128)} copy(f32[8,128,4096]{2,1,0:T(8,128)} %fusion.7) | data formatting | bytes 33554432 | tf_op jit(solution)/shard_map/kis,js->kij/dot_general | solution.py:28
  75.9 2.4 shift_right_arithmetic.20
  78.3 15.2 %multiply_convert_fusion = bf16[8,128,4096]{1,0,2:T(8,128)(2,1)} fusion(f32[8,128,4096]{1,0,2:T(8,128)} %copy.21, bf16[8,128,4096]{1,0,2:T(8,128)(2,1)} %copy.20, s32[8,128,4108]{1,0,2:T(8,128)S(1)} %bitcast.34, s32[4096]{0:T(1024)S(1)} %slice-done), kind=kLoop, calls=%fused_computation.3 | loop fusion | flops 33554432 | bytes 50348032 | tf_op jit(solution)/shard_map/convert_element_type | solution.py:31
  93.5 12.0 %copy.26 = bf16[8,128,4096]{2,1,0:T(8,128)(2,1)} copy(bf16[8,128,4096]{1,0,2:T(8,128)(2,1)} %multiply_convert_fusion) | data formatting | bytes 16777216 | tf_op jit(solution)/shard_map/convert_element_type | solution.py:31
  105.5 7.1 convolution_bitcast_fusion
  112.6 12.0 %copy.33 = bf16[8,4096,128]{2,0,1:T(8,128)(2,1)} copy(bf16[8,4096,128]{1,2,0:T(8,128)(2,1)} %convert_bitcast_fusion) | data formatting | bytes 16777216 | tf_op jit(solution)/shard_map/convert_element_type | solution.py:25
  124.5 8.9 %fusion.4 = f32[4096,128]{1,0:T(8,128)} fusion(f32[4096,128]{1,0:T(8,128)} %convolution_bitcast_fusion, s32[]{:T(128)S(6)} %select_n.4, bf16[8,128,4096]{1,0,2:T(8,128)(2,1)} %multiply_convert_fusion, bf16[8,4096,128]{2,0,1:T(8,128)(2,1)} %copy.33), kind=kOutput, calls=%fused_computation.12 | convolution fusion | flops 1073758208 | bytes 16908292 | tf_op jit(solution)/shard_map/kij,kjr->ir/dot_general | solution.py:32
  133.5 0.0 reduce-scatter.2.cloned.1.call-update
  133.5 0.0 all-reduce.5.cloned.1.call-start
  133.5 6.8 convolution_bitcast_fusion.1
  140.3 0.0 all-reduce.5.cloned.1.call-update
  140.3 0.0 all-reduce.3.cloned.1.call-start
  140.4 207.3 %reduce-scatter.2.cloned.1.call-done = f32[128,128]{1,0:T(8,128)} async-done(((f32[4096,128]{1,0:T(8,128)}), f32[128,128]{1,0:T(8,128)}) %reduce-scatter.2.cloned.1.call-update) | async-done | bytes 65552 | tf_op jit(solution)/shard_map/reduce_scatter | solution.py:40
  347.7 0.0 all-reduce.3.cloned.1.call-update
  347.7 425.6 %all-reduce.5.cloned.1.call-done = f32[8,128,128]{1,2,0:T(8,128)} async-done(((f32[8,128,128]{1,2,0:T(8,128)}), f32[8,128,128]{1,2,0:T(8,128)}) %all-reduce.5.cloned.1.call-update) | async-done | bytes 524304 | tf_op jit(solution)/shard_map/psum | solution.py:45
  773.3 1.1 broadcast_multiply_fusion
  774.4 1.0 copy.28
  775.4 86.1 %all-reduce.3.cloned.1.call-done = f32[128,128]{1,0:T(8,128)} async-done(((f32[128,128]{1,0:T(8,128)}), f32[128,128]{1,0:T(8,128)}) %all-reduce.3.cloned.1.call-update) | async-done | bytes 65552 | tf_op jit(solution)/shard_map/psum | solution.py:41
  861.5 1.5 broadcast_multiply_fusion.1
  (7 shorter events, 0.0 us)
Async XLA Ops:
  7.2 28.6 %copy-start = (bf16[8,128,128]{2,1,0:T(8,128)(2,1)S(1)}, bf16[8,128,128]{2,1,0:T(8,128)(2,1)}, u32[]{:S(2)}) copy-start(bf16[8,128,128]{2,1,0:T(8,128)(2,1)} %param.7) | copy-start | bytes 786436
  9.2 35.6 %all-to-all-start = ((bf16[32,128,128]{2,1,0:T(8,128)(2,1)}), bf16[32,128,128]{2,1,0:T(8,128)(2,1)S(1)}, u32[]{:S(2)}, u32[]{:S(2)}) async-start(bf16[32,128,128]{2,1,0:T(8,128)(2,1)} %stack.2), calls=%async_computation | async-start | bytes 2097152 | tf_op jit(solution)/shard_map/all_to_all | solution.py:23
  23.4 324.2 %reduce-scatter.2.cloned.1.call-start = ((), (), s32[]{:S(2)}) async-start(), calls=%async_computation.2 | async-start | bytes 2162688 | tf_op jit(solution)/shard_map/reduce_scatter | solution.py:40
  23.5 12.3 %copy-start.2 = (bf16[128,128]{1,0:T(8,128)(2,1)S(1)}, bf16[128,128]{1,0:T(8,128)(2,1)}, u32[]{:S(2)}) copy-start(bf16[128,128]{1,0:T(8,128)(2,1)} %param.6) | copy-start | bytes 98308
  35.7 22.7 %copy-start.3 = (s32[4108]{0:T(1024)}, s32[4108]{0:T(1024)S(1)}, u32[]{:S(2)}) copy-start(s32[4108]{0:T(1024)S(1)} %shift_right_arithmetic.23) | copy-start | bytes 49300
  75.9 2.4 slice-start
  124.5 738.4 %copy-start.1 = (bf16[8,128,128]{2,1,0:T(8,128)(2,1)S(1)}, bf16[8,128,128]{2,1,0:T(8,128)(2,1)}, u32[]{:S(2)}) copy-start(bf16[8,128,128]{2,1,0:T(8,128)(2,1)} %param.7) | copy-start | bytes 786436
  133.5 639.9 %all-reduce.5.cloned.1.call-start = ((), (), s32[]{:S(2)}) async-start(), calls=%async_computation.4 | async-start | bytes 1048576 | tf_op jit(solution)/shard_map/psum | solution.py:45
  140.3 721.2 %all-reduce.3.cloned.1.call-start = ((), (), s32[]{:S(2)}) async-start(), calls=%async_computation.3 | async-start | bytes 131072 | tf_op jit(solution)/shard_map/psum | solution.py:41
Sparse Core Ops, SparseCore 0:
  133.6 214.0 reduce-scatter.1
  351.0 422.2 all-reduce.4
  776.0 85.4 all-reduce.2

commit v2 on v0

--- a/solution.py
+++ b/solution.py
@@ -36,7 +36,7 @@
     mine = lax.dynamic_slice_in_dim(all_rows, offset, ent_loc, 0)
     partial_value = lax.dynamic_update_slice_in_dim(all_rows, mine + own_rows, offset, 0)
     shared = lax.psum_scatter(partial_value, "ent", scatter_dimension=0, tiled=True)
-    owned = lax.psum(shared, "rel")
+    owned = jnp.sum(lax.all_gather(shared, "rel"), axis=0)
     grad_factors = owned / jnp.sqrt(jnp.float32(n_all * n_rel))
     pull = pull_sum.astype(jnp.bfloat16)
     core_part = jnp.einsum("ir,kis->krs", factors, pull, preferred_element_type=jnp.float32)

time: 911 us -> 859 us (0.943)
  the two profiles are of different devices: /device:TPU:2 before, /device:TPU:1 now
where the time goes in v2:
time: 859 us; the launch traced here: 858 us
  waiting for transfers between devices  693 us (81%)
  local copies, waits for them, and re-layouts  57.2 us (7%)
  blocking collectives  40.8 us (5%)
  matrix products  36.1 us (4%)
  other arithmetic  16.9 us (2%)
  between operations  13.9 us (2%)
    psum x1, waiting for transfers between devices, per_device(): core_grad = lax.psum(core_part, 'ent')  391 us
    reduce_scatter x1, waiting for transfers between devices, per_device(): lax.psum_scatter(partial_value, 'ent', scatter_dimension=0, tiled=True)  227 us
    all_gather x1, waiting for transfers between devices, per_device(): piece = lax.all_gather(factors, 'ent', axis=0, tiled=True)  74.8 us
    all_gather x1, blocking collectives, per_device(): owned = jnp.sum(lax.all_gather(shared, 'rel'), axis=0)  40.8 us
    dot_general x1, local copies, waits for them, and re-layouts, per_device(): jnp.einsum('kis,js->kij', left, piece, preferred_element_type=jnp.float32)  17.6 us
  transfers between devices with their start and end apart: 3, of which 3 were waited for; matrix products, arithmetic and copies ran while one was open for 3% of the time, Pallas kernels for 0%

profile of v2, /device:TPU:1, one launch (start us, length us, event | category | flops | bytes accessed | tf_op | source)
XLA Modules:
  0.0 857.7 jit_solution(4744611839455099404)
XLA Ops:
  7.2 0.0 copy-start
  7.2 0.0 all-gather.3.cloned.1.call-start
  7.2 0.7 all-gather.3.cloned.1.call-update
  7.9 0.0 all-reduce.2.cloned.1.call-start
  8.0 12.1 %copy.20 = bf16[8,128,4096]{1,0,2:T(8,128)(2,1)} copy(bf16[8,128,4096]{2,1,0:T(8,128)(2,1)} %param.4) | data formatting | bytes 16777216 | tf_op args[0]
  20.1 0.2 shift_right_arithmetic.23
  20.3 0.0 copy-start.7
  20.3 0.3 fusion.2
  20.6 0.0 copy-start.4
  20.6 74.8 %all-gather.3.cloned.1.call-done = bf16[4096,128]{1,0:T(8,128)(2,1)} async-done(((bf16[128,128]{1,0:T(8,128)(2,1)}), bf16[4096,128]{1,0:T(8,128)(2,1)}) %all-gather.3.cloned.1.call-update) | async-done | bytes 1048592 | tf_op jit(solution)/shard_map/all_gather | solution.py:22
  95.4 9.3 %fusion.8 = f32[8,128,4096]{2,1,0:T(8,128)} fusion(bf16[8,128,128]{1,2,0:T(8,128)(2,1)S(1)} %fusion.2, bf16[4096,128]{1,0:T(8,128)(2,1)} %all-gather.3.cloned.1.call-done), kind=kOutput, calls=%fused_computation.15 | convolution fusion | flops 1073741824 | bytes 18087936 | tf_op jit(solution)/shard_map/kis,js->kij/dot_general | solution.py:26
  104.8 0.0 copy-done.7
  104.8 17.6 %copy.21 = f32[8,128,4096]{1,0,2:T(8,128)} copy(f32[8,128,4096]{2,1,0:T(8,128)} %fusion.8) | data formatting | bytes 33554432 | tf_op jit(solution)/shard_map/kis,js->kij/dot_general | solution.py:26
  122.4 1.1 shift_right_arithmetic.20
  123.5 15.2 %multiply_convert_fusion = bf16[8,128,4096]{1,0,2:T(8,128)(2,1)} fusion(f32[8,128,4096]{1,0,2:T(8,128)} %copy.21, bf16[8,128,4096]{1,0,2:T(8,128)(2,1)} %copy.20, s32[8,128,4108]{1,0,2:T(8,128)S(1)} %bitcast.37, s32[4096]{0:T(1024)S(1)} %slice-done), kind=kLoop, calls=%fused_computation.3 | loop fusion | flops 33554432 | bytes 50348032 | tf_op jit(solution)/shard_map/convert_element_type | solution.py:29
  138.6 11.9 %copy.26 = bf16[8,128,4096]{2,1,0:T(8,128)(2,1)} copy(bf16[8,128,4096]{1,0,2:T(8,128)(2,1)} %multiply_convert_fusion) | data formatting | bytes 16777216 | tf_op jit(solution)/shard_map/convert_element_type | solution.py:29
  150.5 5.8 convolution_bitcast_fusion
  156.4 5.6 convert_bitcast_fusion
  162.0 12.0 %copy.33 = bf16[8,4096,128]{2,0,1:T(8,128)(2,1)} copy(bf16[8,4096,128]{1,2,0:T(8,128)(2,1)} %convert_bitcast_fusion) | data formatting | bytes 16777216 | tf_op jit(solution)/shard_map/convert_element_type | solution.py:23
  173.9 6.7 convolution_bitcast_fusion.1
  180.7 0.0 all-reduce.2.cloned.1.call-update
  180.7 0.0 reduce-scatter.2.cloned.1.call-start
  180.7 0.0 copy-start.1
  180.8 8.3 fusion.4
  189.1 1.3 copy-done.2
  190.4 0.0 reduce-scatter.2.cloned.1.call-update
  190.5 390.7 %all-reduce.2.cloned.1.call-done = f32[8,128,128]{1,2,0:T(8,128)} async-done(((f32[8,128,128]{1,2,0:T(8,128)}), f32[8,128,128]{1,2,0:T(8,128)}) %all-reduce.2.cloned.1.call-update) | async-done | bytes 524304 | tf_op jit(solution)/shard_map/psum | solution.py:43
  581.1 1.1 broadcast_multiply_fusion
  582.2 1.0 copy.28
  583.2 226.6 %reduce-scatter.2.cloned.1.call-done = f32[128,128]{1,0:T(8,128)} async-done(((f32[4096,128]{1,0:T(8,128)}), f32[128,128]{1,0:T(8,128)}) %reduce-scatter.2.cloned.1.call-update) | async-done | bytes 65552 | tf_op jit(solution)/shard_map/reduce_scatter | solution.py:38
  809.8 40.8 %all-gather = f32[1024,128]{1,0:T(8,128)S(1)} all-gather(f32[128,128]{1,0:T(8,128)} %reduce-scatter.2.cloned.1.call-done), channel_id=2, replica_groups=mesh['rel'=8,'ent'=32] {'rel'}, dimensions={0}, use_global_device_ids=true | all-gather | bytes 589824 | tf_op jit(solution)/shard_map/all_gather | solution.py:39
  850.6 0.6 broadcast_multiply_fusion.1
  (14 shorter events, 0.1 us)
Async XLA Ops:
  7.2 13.2 %copy-start = (bf16[8,128,128]{2,1,0:T(8,128)(2,1)S(1)}, bf16[8,128,128]{2,1,0:T(8,128)(2,1)}, u32[]{:S(2)}) copy-start(bf16[8,128,128]{2,1,0:T(8,128)(2,1)} %param.7) | copy-start | bytes 786436
  7.2 88.3 %all-gather.3.cloned.1.call-start = ((), (), s32[]{:S(2)}) async-start(), calls=%async_computation.1 | async-start | bytes 1081344 | tf_op jit(solution)/shard_map/all_gather | solution.py:22
  7.9 573.2 %all-reduce.2.cloned.1.call-start = ((), (), s32[]{:S(2)}) async-start(), calls=%async_computation.3 | async-start | bytes 1048576 | tf_op jit(solution)/shard_map/psum | solution.py:43
  8.0 12.4 %copy-start.6 = (bf16[128,128]{1,0:T(8,128)(2,1)S(1)}, bf16[128,128]{1,0:T(8,128)(2,1)}, u32[]{:S(2)}) copy-start(bf16[128,128]{1,0:T(8,128)(2,1)} %param.6) | copy-start | bytes 98308
  20.3 84.5 %copy-start.7 = (s32[4108]{0:T(1024)}, s32[4108]{0:T(1024)S(1)}, u32[]{:S(2)}) copy-start(s32[4108]{0:T(1024)S(1)} %shift_right_arithmetic.23) | copy-start | bytes 49300
  20.6 84.2 %copy-start.4 = (bf16[8,128,128]{1,2,0:T(8,128)(2,1)}, bf16[8,128,128]{1,2,0:T(8,128)(2,1)S(1)}, u32[]{:S(2)}) copy-start(bf16[8,128,128]{1,2,0:T(8,128)(2,1)S(1)} %fusion.2) | copy-start | bytes 786436
  104.8 17.6 %copy-start.5 = (s32[8,128,316]{1,0,2:T(8,128)S(1)}, s32[8,128,316]{1,0,2:T(8,128)}, u32[]{:S(2)}) copy-start(s32[8,128,316]{1,0,2:T(8,128)} %param.5) | copy-start | bytes 3883012
  122.4 1.1 slice-start
  150.5 5.9 copy-start.3
  180.7 629.1 %reduce-scatter.2.cloned.1.call-start = ((), (), s32[]{:S(2)}) async-start(), calls=%async_computation.2 | async-start | bytes 2162688 | tf_op jit(solution)/shard_map/reduce_scatter | solution.py:38
  180.7 670.5 %copy-start.1 = (bf16[8,128,128]{2,1,0:T(8,128)(2,1)S(1)}, bf16[8,128,128]{2,1,0:T(8,128)(2,1)}, u32[]{:S(2)}) copy-start(bf16[8,128,128]{2,1,0:T(8,128)(2,1)} %param.7) | copy-start | bytes 786436
  189.1 1.3 copy-start.2
Sparse Core Ops, SparseCore 0:
  11.4 83.9 all-gather.2
  180.8 400.2 all-reduce.1
  583.8 225.9 reduce-scatter.1
